TPU v7x, 128 devices: a whole 4x4x4 slice. The times are simulated.
128 devices in a mesh: layer: 4 (over y_hi, core), tok: 32 (over y_lo, z, x).
Axes of the slice: x: 4, y: 4 (y_hi: 2, y_lo: 2; y = y_hi * 2 + y_lo), z: 4, core: 2. Of those that a mesh axis runs over, the one named last changes fastest.
Arguments:
- inputs: bfloat16 [8, 20480, 4096], P('layer', 'tok'), may hold values from -6 to 6
- out_grads: bfloat16 [8, 20480, 4096], P('layer', 'tok'), may hold values from -6 to 6
- a_inverse: bfloat16 [8, 4096, 4096], P('layer', None, 'tok')
- g_inverse: bfloat16 [8, 4096, 4096], P('layer', None, 'tok')
- query_in: bfloat16 [8, 32, 8, 4096], P('layer', None, None, 'tok'), may hold values from -0.03125 to 0.03125
- query_out: bfloat16 [8, 32, 8, 4096], P('layer', None, None, 'tok'), may hold values from -0.03125 to 0.03125
Outputs:
- scores: float32 [20480, 32], P('tok', 'layer')
All inputs are finite; a program needn't handle non-finite values.
Results may differ from a plain program's by a relative error of at most 0.0041.
Values may be sent and summed in bfloat16 or wider, within the bound.
A program may use at most 128 MiB of HBM per device.

v0:
```python
import jax
import jax.numpy as jnp
from jax import lax
from jax.sharding import PartitionSpec as P


def precondition(factors, inverse):
    return jnp.einsum("qrj,ij->qri", factors, inverse, preferred_element_type=jnp.float32)


def local(inputs, out_grads, a_inverse, g_inverse, query_in, query_out):
    layers_here = inputs.shape[0]
    width = a_inverse.shape[1]
    rank = query_in.shape[2]
    queries = query_in.shape[1]
    half = layers_here * rank * width
    side_in = jnp.stack(
        [precondition(query_in[k], a_inverse[k]) for k in range(layers_here)], axis=1
    )
    side_out = jnp.stack(
        [precondition(query_out[k], g_inverse[k]) for k in range(layers_here)], axis=1
    )
    summed = lax.psum(
        jnp.concatenate([side_in.reshape(queries, half), side_out.reshape(queries, half)], axis=1),
        "tok",
    ).astype(jnp.bfloat16)
    pre_in = summed[:, :half].reshape(queries, layers_here, rank, width)
    pre_out = summed[:, half:].reshape(queries, layers_here, rank, width)
    partial_sum = jnp.zeros((inputs.shape[1], pre_in.shape[0]), jnp.float32)
    for k in range(layers_here):
        side_in = jnp.einsum(
            "td,qrd->tqr", inputs[k], pre_in[:, k], preferred_element_type=jnp.float32
        )
        side_out = jnp.einsum(
            "td,qrd->tqr", out_grads[k], pre_out[:, k], preferred_element_type=jnp.float32
        )
        partial_sum = partial_sum + jnp.sum(side_in * side_out, axis=2)
    return lax.psum_scatter(partial_sum, "layer", scatter_dimension=1, tiled=True)


def solution(mesh):
    in_specs = (
        P("layer", "tok", None),
        P("layer", "tok", None),
        P("layer", None, "tok"),
        P("layer", None, "tok"),
        P("layer", None, None, "tok"),
        P("layer", None, None, "tok"),
    )
    out_specs = P("tok", "layer")
    return jax.shard_map(local, mesh=mesh, in_specs=in_specs, out_specs=out_specs, check_vma=False)
```

profile of v0, /device:TPU:1, one launch (start us, length us, event | category | flops | bytes accessed | tf_op | source)
XLA Modules:
  0.0 480.2 jit_solution(14431003502886575436)
XLA Ops:
  6.5 0.0 copy-start.3
  6.5 0.0 all-reduce.4.cloned.1.call-start
  6.5 2.1 convolution_bitcast_fusion.2
  8.7 0.0 copy-done.3
  8.7 0.0 copy-done.1
  8.7 0.7 convolution_bitcast_fusion.3
  9.4 0.0 copy-done.4
  9.4 0.0 copy-done.2
  9.4 0.7 convolution_bitcast_fusion
  10.1 2.7 convolution_bitcast_fusion.1
  12.8 1.0 pad_maximum_fusion.1
  13.8 1.0 copy.13
  14.8 0.0 copy-start
  14.8 8.1 %copy.23 = f32[4,8,16,4096]{3,1,2,0:T(8,128)} copy(f32[4,8,16,4096]{3,2,1,0:T(8,128)S(1)} %bitcast.103) | data formatting | bytes 16777216
  22.9 0.0 copy-done
  22.9 1.0 pad_maximum_fusion.2
  23.9 1.0 copy.14
  24.9 0.0 slice-start
  24.9 0.0 slice-start.1
  24.9 8.3 %copy.24 = f32[4,8,16,4096]{3,1,2,0:T(8,128)} copy(f32[4,8,16,4096]{3,2,1,0:T(8,128)S(1)} %bitcast.104) | data formatting | bytes 16777216
  33.2 0.0 slice-done
  33.2 0.0 slice-done.1
  33.2 9.4 %pad_maximum_fusion = f32[32,131072]{1,0:T(8,128)} fusion(f32[32,65536]{1,0:T(8,128)} %bitcast.108, f32[32,65536]{1,0:T(8,128)S(1)} %bitcast.107), kind=kLoop, calls=%fused_computation | loop fusion | flops 4194304 | bytes 33554432 | tf_op jit(solution)/shard_map/concatenate | solution.py:24
  42.6 370.7 %all-reduce.5 = bf16[32,131072]{1,0:T(8,128)(2,1)} all-reduce(f32[32,131072]{1,0:T(8,128)} %pad_maximum_fusion), channel_id=1, replica_groups=mesh['layer'=4,'tok'=32] {'tok'}, use_global_device_ids=true, to_apply=%region_0.0 | all-reduce | flops 4194304 | bytes 25165824 | tf_op jit(solution)/shard_map/psum | solution.py:23
  413.3 3.9 fusion.40
  417.2 0.0 slice-start.4
  417.2 2.3 copy.26
  419.6 0.0 slice-done.2
  419.6 0.0 slice-done.3
  419.6 0.4 slice-done.4
  420.0 1.9 fusion
  421.9 0.0 slice-start.5
  421.9 0.0 slice-start.6
  421.9 1.9 fusion.4
  423.8 0.0 slice-start.7
  423.9 2.3 copy.25
  426.2 0.0 slice-done.5
  426.2 0.0 slice-done.6
  426.2 0.0 slice-done.7
  426.3 1.9 fusion.18
  428.2 0.0 copy-start.5
  428.2 2.0 fusion.21
  430.2 0.6 add_bitcast_fusion
  430.8 0.0 all-reduce.4.cloned.1.call-update
  430.9 0.0 copy-done.5
  430.9 0.6 dynamic-slice
  432.1 39.9 %all-reduce.4.cloned.1.call-done = f32[640,32]{0,1:T(8,128)} async-done(((f32[640,32]{0,1:T(8,128)}), f32[640,32]{0,1:T(8,128)}) %all-reduce.4.cloned.1.call-update) | async-done | bytes 81936
  472.0 1.3 constant_dynamic-slice_fusion
  (8 shorter events, 0.0 us)
Async XLA Ops:
  6.5 2.1 copy-start.3
  6.5 2.1 copy-start.1
  6.5 2.9 copy-start.4
  6.5 465.5 %all-reduce.4.cloned.1.call-start = ((), (), s32[]{:S(2)}) async-start(), calls=%async_computation | async-start | bytes 163840
  6.5 2.9 copy-start.2
  14.8 8.1 %copy-start = (f32[32,1,8,4096]{3,2,0,1:T(8,128)S(1)}, f32[32,1,8,4096]{3,2,0,1:T(8,128)}, u32[]{:S(2)}) copy-start(f32[32,1,8,4096]{3,2,0,1:T(8,128)} %convolution_bitcast_fusion.1) | copy-start | bytes 12582916
  24.9 8.3 %slice-start = ((s8[8388608]{0:T(1024)(128)(4,1)}), s8[4194304]{0:T(1024)(128)(4,1)S(1)}, s32[]{:S(2)}) async-start(s8[8388608]{0:T(1024)(128)(4,1)} %bitcast.105), calls=%async_computation.1 | async-start | bytes 8388608
  24.9 8.3 %slice-start.1 = ((s8[8388608]{0:T(1024)(128)(4,1)}), s8[4194304]{0:T(1024)(128)(4,1)S(1)}, s32[]{:S(2)}) async-start(s8[8388608]{0:T(1024)(128)(4,1)} %bitcast.105), calls=%async_computation.2 | async-start | bytes 8388608
  413.3 6.3 %slice-start.2 = ((s8[10485760]{0:T(1024)(128)(4,1)}), s8[4194304]{0:T(1024)(128)(4,1)S(1)}, s32[]{:S(2)}) async-start(s8[10485760]{0:T(1024)(128)(4,1)} %bitcast.115), calls=%async_computation.3 | async-start | bytes 8388608
  413.3 6.3 %slice-start.3 = ((s8[10485760]{0:T(1024)(128)(4,1)}), s8[4194304]{0:T(1024)(128)(4,1)S(1)}, s32[]{:S(2)}) async-start(s8[10485760]{0:T(1024)(128)(4,1)} %bitcast.115), calls=%async_computation.4 | async-start | bytes 8388608
  417.2 2.8 slice-start.4
  421.9 4.3 slice-start.5
  421.9 4.3 slice-start.6
  423.8 2.4 slice-start.7
  428.2 2.6 copy-start.5
Sparse Core Ops, SparseCore 0:
  431.0 40.9 all-reduce.3
where the time goes:
time: 480 us
  blocking collectives  371 us (77%)
  waiting for transfers between devices  39.9 us (8%)
  local copies, waits for them, and re-layouts  29.4 us (6%)
  between operations  14.3 us (3%)
  matrix products  13.9 us (3%)
  other arithmetic  12 us (2%)
    psum x1, blocking collectives, local(): lax.psum(jnp.concatenate([side_in.reshape(queries, half), side_out.reshap...  371 us
    unnamed x2, waiting for transfers between devices  39.9 us
    unnamed x34, local copies, waits for them, and re-layouts  23.5 us
  transfers between devices with their start and end apart: 1, of which 1 were waited for; matrix products, arithmetic and copies ran while one was open for 0% of the time, Pallas kernels for 0%

commit v1 on v0

v1 whole, which is shorter than its diff:
```python
import functools

import jax
import jax.numpy as jnp
from jax import lax
from jax.experimental import pallas as pl
from jax.experimental.pallas import tpu as pltpu
from jax.sharding import PartitionSpec as P

MESH = pl.DeviceIdType.MESH
BF16, F32 = jnp.bfloat16, jnp.float32
SCALE = 2.0**29
NT = (((1,), (1,)), ((), ()))
SLABS = 4


def encode(v):
    a = v * jnp.abs(v)
    return (a * jnp.abs(a)).astype(BF16)


def decode(code):
    w = code.astype(F32)
    r = lax.rsqrt(jnp.maximum(jnp.abs(w), 1e-37))
    return w * (r * r * lax.rsqrt(r))


def order():
    todo = []
    for s in range(SLABS):
        for k in range(11):
            for b in range(2):
                todo.append((START[s] + GAP[k], s, b, k))
    return [(s, b, k) for _, s, b, k in sorted(todo)]


START = (0, 8, 16, 24)
GAP = (0, 4, 6, 8, 9.5, 11, 12.5, 14, 15.5, 20, 23)


def kernel(
    q_ref, a_hbm, g_hbm, x_hbm, o_hbm, out_ref,
    qs, fac, inp, part_a, part_b, pre_a, pre_b,
    rp_a, rs_a, ry_a, ry_b, rs_b, rp_b,
    sp_a, ss_a, sy_a, sy_b, ss_b, sp_b,
    side, fin, rfin,
    fac_sem, inp_sem, send_sem, recv_sem, fin_send, fin_recv,
):
    lay, tok = lax.axis_index("layer"), lax.axis_index("tok")
    core = lay % 2
    y = tok // 16
    step_p, step_s = 1 + 3 * core, 4 - 3 * core
    p, s = (tok // step_p) % 4, (tok // step_s) % 4
    ha, qb = part_a.shape[-1], part_b.shape[-1]
    wa = 2 * ha

    def at(p_, s_, y_):
        return (lay, y_ * 16 + p_ * step_p + s_ * step_s)

    right_p, left_p = at((p + 1) % 4, s, y), at((p + 3) % 4, s, y)
    right_s, left_s = at(p, (s + 1) % 4, y), at(p, (s + 3) % 4, y)
    across = at(p, s, 1 - y)
    peers = [((lay + d) % 4, tok) for d in (1, 2, 3)]

    def fac_copy(k):
        src = (a_hbm, g_hbm)[k % 2]
        return pltpu.make_async_copy(src.at[k // 2], fac.at[k], fac_sem.at[k])

    def inp_copy(k):
        src = (x_hbm, o_hbm)[k % 2]
        return pltpu.make_async_copy(src.at[k // 2], inp.at[k % 2], inp_sem.at[k])

    for k in range(SLABS):
        fac_copy(k).start()
    for k in range(2):
        inp_copy(k).start()

    barrier = pltpu.get_barrier_semaphore()
    everyone = [right_p, left_p, right_s, left_s, across, *peers]
    for who in everyone:
        pl.semaphore_signal(barrier, inc=1, device_id=who, device_id_type=MESH)

    qs[...] = q_ref[...] * jnp.asarray(SCALE, BF16)

    def partial_products(k):
        def tile(dst, row, width):
            dst[...] = lax.dot_general(
                qs[k], fac[k, pl.ds(row, width), :], NT, preferred_element_type=F32
            )

        for h in range(2):
            for c in range(0, ha, 512):
                tile(part_a.at[k, h, :, pl.ds(c, 512)], h * ha + c, 512)
        for h in range(4):
            tile(part_b.at[k, h // 2, h % 2], wa + h * qb, qb)

    def remote(k, b, n, src, dst, who):
        return pltpu.make_async_remote_copy(
            src_ref=src, dst_ref=dst, send_sem=send_sem.at[k, b, n], recv_sem=recv_sem.at[k, b, n],
            device_id=who, device_id_type=MESH,
        )

    def rows_loop(n, body):
        if n == 16:
            body(0)
        else:
            pl.loop(0, n // 16)(lambda i: body(pl.multiple_of(i * 16, 16)))

    def put(dst, src, row0, n, more=None):
        def body(r):
            v = src[pl.ds(pl.multiple_of(row0 + r, 16), 16), :]
            if more is not None:
                v = v + decode(more[pl.ds(r, 16), :])
            dst[pl.ds(r, 16), :] = encode(v)

        rows_loop(n, body)

    def add(src, row0, n, one, two=None):
        def body(r):
            rows = pl.ds(pl.multiple_of(row0 + r, 16), 16)
            v = src[rows, :] + decode(one[pl.ds(r, 16), :])
            if two is not None:
                v = v + decode(two[pl.ds(r, 16), :])
            src[rows, :] = v

        rows_loop(n, body)

    class Scatter:
        def __init__(self, k, b, base, halves, sent, got, row0, n, me, right, left):
            self.__dict__.update(locals())

        def copy(self, m):
            who = self.left if m % 2 else self.right
            return remote(self.k, self.b, self.base + m, self.sent.at[m], self.got.at[m], who)

        def row(self, d):
            return self.row0 + (self.me + d) % 4 * self.n

        def first(self):
            lo, hi = self.halves
            for m, (src, d) in enumerate(((hi, 2), (lo, 2), (lo, 1), (hi, 3))):
                put(self.sent.at[m], src, self.row(d), self.n)
                self.copy(m).start()

        def second(self):
            lo, hi = self.halves
            for m, (src, d) in enumerate(((hi, 1), (lo, 3))):
                self.copy(m).wait_recv()
                put(self.sent.at[4 + m], src, self.row(d), self.n, self.got.at[m])
                self.copy(4 + m).start()

        def last(self):
            lo, hi = self.halves
            for m in (2, 3, 4, 5):
                self.copy(m).wait_recv()
            add(lo, self.row(0), self.n, self.got.at[2], self.got.at[5])
            add(hi, self.row(0), self.n, self.got.at[3], self.got.at[4])

        def sends(self):
            return [self.copy(m) for m in range(6)]

    class Gather:
        def __init__(self, k, b, base, halves, row0, n, me, right, left):
            self.__dict__.update(locals())

        def copy(self, m):
            half = self.halves[(1, 0, 0, 1, 1, 0)[m]]
            d = (0, 0, 0, 0, 3, 1)[m]
            ref = half.at[pl.ds(pl.multiple_of(self.row0 + (self.me + d) % 4 * self.n, 16), self.n), :]
            return remote(self.k, self.b, self.base + m, ref, ref, self.left if m % 2 else self.right)

        def first(self):
            for m in range(4):
                self.copy(m).start()

        def second(self):
            for m in range(2):
                self.copy(m).wait_recv()
                self.copy(4 + m).start()

        def last(self):
            for m in (2, 3, 4, 5):
                self.copy(m).wait_recv()

        def sends(self):
            return [self.copy(m) for m in range(6)]

    def final_rows(dst, src, row0, n, got):
        rows = pl.ds(pl.multiple_of(row0, 16), n)
        dst[rows, :] = ((src[rows, :] + decode(got)) * (1.0 / SCALE)).astype(BF16)

    def ay_copy(k):
        return remote(k, 0, 12, sy_a.at[k], ry_a.at[k], across)

    def agy_copy(k):
        block = pre_a.at[k, y, pl.ds(pl.multiple_of(64 * p + 16 * s, 16), 16), :]
        return remote(k, 0, 13, block, block, across)

    def by_copy(k):
        return remote(k, 1, 12, sy_b.at[k], ry_b.at[k], across)

    def bgy_copy(k):
        block = pre_b.at[k, y]
        return remote(k, 1, 13, block, block, across)

    stage = {}
    for k in range(SLABS):
        ha_refs = [part_a.at[k, h] for h in range(2)]
        hb_refs = [part_b.at[k, y, h] for h in range(2)]
        ga_refs = [pre_a.at[k, h] for h in range(2)]
        gb_refs = [pre_b.at[k, y, h] for h in range(2)]
        stage[k] = dict(
            ap=Scatter(k, 0, 0, ha_refs, sp_a.at[k], rp_a.at[k], 0, 64, p, right_p, left_p),
            as_=Scatter(k, 0, 6, ha_refs, ss_a.at[k], rs_a.at[k], 64 * p, 16, s, right_s, left_s),
            ags=Gather(k, 0, 14, ga_refs, 64 * p, 16, s, right_s, left_s),
            agp=Gather(k, 0, 20, ga_refs, 0, 64, p, right_p, left_p),
            bs=Scatter(k, 1, 0, hb_refs, ss_b.at[k], rs_b.at[k], 0, 64, s, right_s, left_s),
            bp=Scatter(k, 1, 6, hb_refs, sp_b.at[k], rp_b.at[k], 64 * s, 16, p, right_p, left_p),
            bgp=Gather(k, 1, 14, gb_refs, 64 * s, 16, p, right_p, left_p),
            bgs=Gather(k, 1, 20, gb_refs, 0, 64, s, right_s, left_s),
        )

    def score(k, piece, first):
        acc = side.at[k % 2]
        data = inp.at[k % 2]

        def go(pre, col, width, init):
            v = lax.dot_general(data[:, pl.ds(col, width)], pre, NT, preferred_element_type=F32)
            acc[...] = v if init else acc[...] + v

        if piece == 0:
            for h in range(2):
                for c in range(0, ha, 512):
                    go(pre_a[k, h, :, pl.ds(c, 512)], h * ha + c, 512, first and h == 0 and c == 0)
        else:
            for h in range(4):
                go(pre_b[k, h // 2, h % 2], wa + h * qb, qb, first and h == 0)

    done = {}

    def finish(k, b):
        if k not in done:
            inp_copy(k).wait()
        score(k, b, k not in done)
        done[k] = done.get(k, 0) + 1
        if done[k] < 2:
            return
        if k + 2 < SLABS:
            inp_copy(k + 2).start()
        if k % 2:
            pick = jnp.where(
                lax.broadcasted_iota(jnp.int32, (32, 256), 1) // 8
                == lax.broadcasted_iota(jnp.int32, (32, 256), 0),
                1.0, 0.0,
            ).astype(BF16)
            for t in range(0, side.shape[1], 128):
                prod = side[0, pl.ds(t, 128), :] * side[1, pl.ds(t, 128), :]
                total = None
                for _ in range(3):
                    top = prod.astype(BF16)
                    prod = prod - top.astype(F32)
                    part = lax.dot_general(pick, top, NT, preferred_element_type=F32)
                    total = part if total is None else total + part
                fin[:, pl.ds(t, 128)] = total if k == 1 else fin[:, pl.ds(t, 128)] + total

    def a_step(k, n):
        g = stage[k]
        if n == 0:
            g["ap"].first()
        elif n == 1:
            g["ap"].second()
        elif n == 2:
            g["ap"].last()
            g["as_"].first()
        elif n == 3:
            g["as_"].second()
        elif n == 4:
            g["as_"].last()
            put(sy_a.at[k], part_a.at[k, 1 - y], 64 * p + 16 * s, 16)
            ay_copy(k).start()
        elif n == 5:
            ay_copy(k).wait_recv()
            final_rows(pre_a.at[k, y], part_a.at[k, y], 64 * p + 16 * s, 16, ry_a[k])
            agy_copy(k).start()
        elif n == 6:
            agy_copy(k).wait_recv()
            g["ags"].first()
        elif n == 7:
            g["ags"].second()
        elif n == 8:
            g["ags"].last()
            g["agp"].first()
        elif n == 9:
            g["agp"].second()
        else:
            g["agp"].last()
            finish(k, 0)

    def b_step(k, n):
        g = stage[k]
        if n == 0:
            for h in range(2):
                put(sy_b.at[k, h], part_b.at[k, 1 - y, h], 0, 256)
            by_copy(k).start()
        elif n == 1:
            by_copy(k).wait_recv()
            for h in range(2):
                add(part_b.at[k, y, h], 0, 256, ry_b.at[k, h])
            g["bs"].first()
        elif n == 2:
            g["bs"].second()
        elif n == 3:
            g["bs"].last()
            g["bp"].first()
        elif n == 4:
            g["bp"].second()
        elif n == 5:
            g["bp"].last()
            rows = pl.ds(pl.multiple_of(64 * s + 16 * p, 16), 16)
            for h in range(2):
                pre_b[k, y, h, rows, :] = (part_b[k, y, h, rows, :] * (1.0 / SCALE)).astype(BF16)
            g["bgp"].first()
        elif n == 6:
            g["bgp"].second()
        elif n == 7:
            g["bgp"].last()
            g["bgs"].first()
        elif n == 8:
            g["bgs"].second()
        elif n == 9:
            g["bgs"].last()
            bgy_copy(k).start()
        else:
            bgy_copy(k).wait_recv()
            finish(k, 1)

    met = False
    for k, b, n in order():
        if b == 0 and n == 0:
            fac_copy(k).wait()
            partial_products(k)
            if not met:
                pl.semaphore_wait(barrier, len(everyone))
                met = True
        (a_step, b_step)[b](k, n)

    def fin_copy(d):
        who = (lay + d) % 4
        return pltpu.make_async_remote_copy(
            src_ref=fin.at[pl.ds(pl.multiple_of(8 * who, 8), 8), :], dst_ref=rfin.at[d - 1],
            send_sem=fin_send.at[d - 1], recv_sem=fin_recv.at[d - 1],
            device_id=(who, tok), device_id_type=MESH,
        )

    for d in (2, 3, 1):
        fin_copy(d).start()
    for k in range(SLABS):
        g = stage[k]
        for ring in g.values():
            for c in ring.sends():
                c.wait_send()
        for c in (ay_copy(k), agy_copy(k), by_copy(k), bgy_copy(k)):
            c.wait_send()
    total = fin[pl.ds(pl.multiple_of(8 * lay, 8), 8), :]
    for d in (1, 2, 3):
        fin_copy(d).wait()
        total = total + rfin[d - 1]
    out_ref[...] = total


def local(inputs, out_grads, a_inverse, g_inverse, query_in, query_out):
    layers, tokens, width = inputs.shape
    depth = a_inverse.shape[2]
    rows = query_in.shape[1] * query_in.shape[2]
    wb = 1024
    ha, qb = (width - wb) // 2, wb // 4
    q = jnp.stack([query_in, query_out], axis=1).reshape(SLABS, rows, depth)
    vmem = pltpu.VMEM
    dma = pltpu.SemaphoreType.DMA
    coded = [
        vmem((SLABS, 6, 64, ha), BF16), vmem((SLABS, 6, 16, ha), BF16), vmem((SLABS, 16, ha), BF16),
        vmem((SLABS, 2, rows, qb), BF16), vmem((SLABS, 6, 64, qb), BF16), vmem((SLABS, 6, 16, qb), BF16),
    ]
    hbm = pl.BlockSpec(memory_space=pl.ANY)
    scores = pl.pallas_call(
        kernel,
        out_shape=jax.ShapeDtypeStruct((8, tokens), F32),
        in_specs=[pl.BlockSpec(memory_space=pltpu.VMEM), hbm, hbm, hbm, hbm],
        out_specs=pl.BlockSpec(memory_space=pltpu.VMEM),
        scratch_shapes=[
            vmem((SLABS, rows, depth), BF16),
            vmem((SLABS, width, depth), BF16),
            vmem((2, tokens, width), BF16),
            vmem((SLABS, 2, rows, ha), F32),
            vmem((SLABS, 2, 2, rows, qb), F32),
            vmem((SLABS, 2, rows, ha), BF16),
            vmem((SLABS, 2, 2, rows, qb), BF16),
            *coded, *coded,
            vmem((2, tokens, rows), F32),
            vmem((32, tokens), F32),
            vmem((3, 8, tokens), F32),
            dma((SLABS,)), dma((SLABS,)),
            dma((SLABS, 2, 26)), dma((SLABS, 2, 26)),
            dma((3,)), dma((3,)),
        ],
        compiler_params=pltpu.CompilerParams(
            collective_id=1, has_side_effects=True, vmem_limit_bytes=60 * 2**20
        ),
        cost_estimate=pl.CostEstimate(flops=6 * 10**9, bytes_accessed=26 * 10**6, transcendentals=0),
        name="influence",
    )(q, a_inverse, g_inverse, inputs, out_grads)
    return scores.T


def solution(mesh):
    in_specs = (
        P("layer", "tok", None),
        P("layer", "tok", None),
        P("layer", None, "tok"),
        P("layer", None, "tok"),
        P("layer", None, None, "tok"),
        P("layer", None, None, "tok"),
    )
    return jax.shard_map(
        local, mesh=mesh, in_specs=in_specs, out_specs=P("tok", "layer"), check_vma=False
    )
```

time: 480 us -> 147 us (0.31)
  blocking collectives: 371 us -> 0 us
  Pallas kernels: 0 us -> 144 us
  waiting for transfers between devices: 39.9 us -> 0 us
  local copies, waits for them, and re-layouts: 29.4 us -> 2.05 us
  between operations: 14.3 us -> 0.01 us
  matrix products: 13.9 us -> 0 us
  other arithmetic: 12 us -> 0.99 us
    psum x1 -> x0, blocking collectives: 371 us -> none  [local(): lax.psum(jnp.concatenate([side_in.reshape(queries, half), side_out.reshap...]
    pallas_call x0 -> x1, Pallas kernels: none -> 144 us  [local(): pl.pallas_call(kernel, out_shape=jax.ShapeDtypeStruct((8, tokens), F32),...]
    unnamed x2 -> x0, waiting for transfers between devices: 39.9 us -> none
    unnamed x34 -> x1, local copies, waits for them, and re-layouts: 23.5 us -> 1.34 us
    dot_general x8 -> x0, matrix products: 13.9 us -> none  [the longest x4 6.21 us: precondition(): jnp.einsum('qrj,ij->qri', factors, inverse, preferred_element_type=jnp.fl...]
    concatenate x1 -> x0, other arithmetic: 9.44 us -> none  [local(): jnp.concatenate([side_in.reshape(queries, half), side_out.reshape(queries...]
  transfers between devices with their start and end apart: 1 -> 0, of which waited for: 1 -> 0; matrix products, arithmetic and copies ran while one was open for 0% -> 0% of each run, Pallas kernels for 0% -> 0%
where the time goes in v1:
time: 147 us
  Pallas kernels  144 us (98%)
  local copies, waits for them, and re-layouts  2.05 us (1%)
    pallas_call x1, Pallas kernels, local(): pl.pallas_call(kernel, out_shape=jax.ShapeDtypeStruct((8, tokens), F32),...  144 us

profile of v1, /device:TPU:1, one launch (start us, length us, event | category | flops | bytes accessed | tf_op | source)
XLA Modules:
  0.0 147.1 jit_solution(11533804899207489163)
XLA Ops:
  0.0 1.0 pad_maximum_fusion
  1.0 0.7 copy.7
  1.7 144.1 %influence.1 = f32[8,640]{1,0:T(8,128)} custom-call(bf16[4,256,128]{2,1,0:T(8,128)(2,1)} %bitcast.4, bf16[2,4096,128]{2,1,0:T(8,128)(2,1)} %a_hbm.1, bf16[2,4096,128]{2,1,0:T(8,128)(2,1)} %g_hbm.1, bf16[2,640,4096]{2,1,0:T(8,128)(2,1)} %x_hbm.1, bf16[2,640,4096]{2,1,0:T(8,128)(2,1)} %o_hbm.1), custom_call_target="tpu_custom_call" | custom-call | flops 6000000000 | bytes 26000000 | tf_op jit(solution)/shard_map/influence/pallas_call | solution.py:385
  145.8 1.3 copy.9

commit v2 on v0

v2 whole, which is shorter than its diff:
```python
import jax
import jax.numpy as jnp
from jax import lax
from jax.experimental import pallas as pl
from jax.experimental.pallas import tpu as pltpu
from jax.sharding import PartitionSpec as P

MESH = pl.DeviceIdType.MESH
BF16, F32 = jnp.bfloat16, jnp.float32
SCALE = 2.0**29
NT = (((1,), (1,)), ((), ()))
SLABS = 4
WEST, EAST = 3, 1

UNITS = (
    (0, 0, 0, 3072),
    (0, 1, 3072, 1024),
    (1, 0, 0, 2048),
    (1, 1, 2048, 1024),
    (1, 2, 3072, 1024),
    (2, 0, 0, 2048),
    (2, 1, 2048, 1024),
    (2, 2, 3072, 1024),
    (3, 0, 0, 2048),
    (3, 1, 2048, 1024),
    (3, 2, 3072, 1024),
)

ORDER = (
    0, 1, 2, 3, 4, 5, 6, 7, 8, 9, 10, 0, 1, 2, 1, 3, 5, 1, 4, 3, 8, 6, 3, 0, 2, 5, 6, 1, 4, 7,
    0, 2, 8, 9, 5, 3, 1, 4, 6, 7, 0, 2, 8, 10, 9, 3, 5, 1, 6, 7, 4, 8, 10, 0, 9, 3, 2, 1, 7, 4,
    5, 6, 10, 0, 8, 3, 9, 2, 7, 5, 6, 10, 0, 8, 2, 9, 5, 1, 4, 6, 10, 8, 9, 4, 0, 3, 7, 9, 4, 2,
    7, 5, 6, 10, 7, 8, 10, 9, 0, 4, 10, 2, 5, 7, 8, 4, 10, 7, 10,
)


def encode(v):
    a = v * jnp.abs(v)
    return (a * jnp.abs(a)).astype(BF16)


def decode(code):
    w = code.astype(F32)
    r = lax.rsqrt(jnp.maximum(jnp.abs(w), 1e-37))
    return w * (r * r * lax.rsqrt(r))


def aligned(row):
    return row if isinstance(row, int) else pl.multiple_of(row, 16)


class Remote:
    def __init__(self, log, sems, n, src, dst, who):
        self.log = log
        self.copy = pltpu.make_async_remote_copy(
            src_ref=src, dst_ref=dst, send_sem=sems[0].at[n], recv_sem=sems[1].at[n],
            device_id=who, device_id_type=MESH,
        )

    def start(self):
        self.copy.start()
        self.log.append(self.copy)

    def wait(self):
        self.copy.wait_recv()


def rows_loop(n, body):
    if n == 16:
        body(0)
    else:
        pl.loop(0, n // 16)(lambda i: body(pl.multiple_of(i * 16, 16)))


def put(dst, src, row0, n, more=None):
    def body(r):
        v = src[pl.ds(aligned(row0 + r), 16), :]
        if more is not None:
            v = v + decode(more[pl.ds(r, 16), :])
        dst[pl.ds(r, 16), :] = encode(v)

    rows_loop(n, body)


def add(src, row0, n, *coded):
    def body(r):
        rows = pl.ds(aligned(row0 + r), 16)
        v = src[rows, :]
        for c in coded:
            v = v + decode(c[pl.ds(r, 16), :])
        src[rows, :] = v

    rows_loop(n, body)


class Scatter:
    def __init__(self, remote, base, halves, sent, got, row0, n, me, ring):
        self.__dict__.update(locals())

    def copy(self, m):
        return self.remote(self.base + m, self.sent.at[m], self.got.at[m], self.ring[EAST if m % 2 == 0 else WEST])

    def row(self, d):
        return self.row0 + (self.me + d) % 4 * self.n

    def first(self):
        lo, hi = self.halves
        for m, (src, d) in enumerate(((hi, 2), (lo, 2), (lo, 1), (hi, 3))):
            put(self.sent.at[m], src, self.row(d), self.n)
            self.copy(m).start()

    def second(self):
        lo, hi = self.halves
        for m, (src, d) in enumerate(((hi, 1), (lo, 3))):
            self.copy(m).wait()
            put(self.sent.at[4 + m], src, self.row(d), self.n, self.got.at[m])
            self.copy(4 + m).start()

    def last(self):
        lo, hi = self.halves
        for m in (2, 3, 4, 5):
            self.copy(m).wait()
        add(lo, self.row(0), self.n, self.got.at[2], self.got.at[5])
        add(hi, self.row(0), self.n, self.got.at[3], self.got.at[4])


class Gather:
    def __init__(self, remote, base, halves, row0, n, me, ring):
        self.__dict__.update(locals())

    def copy(self, m):
        half = self.halves[(1, 0, 0, 1, 1, 0)[m]]
        d = (0, 0, 0, 0, 3, 1)[m]
        ref = half.at[pl.ds(aligned(self.row0 + (self.me + d) % 4 * self.n), self.n), :]
        return self.remote(self.base + m, ref, ref, self.ring[EAST if m % 2 == 0 else WEST])

    def first(self):
        for m in range(4):
            self.copy(m).start()

    def second(self):
        for m in range(2):
            self.copy(m).wait()
            self.copy(4 + m).start()

    def last(self):
        for m in (2, 3, 4, 5):
            self.copy(m).wait()


class Direct:
    def __init__(self, remote, base, halves, sent, got, row0, n, me, ring):
        self.__dict__.update(locals())

    def copy(self, m):
        return self.remote(self.base + m, self.sent.at[m], self.got.at[m], self.ring[(2, 1, 3)[m]])

    def first(self):
        for m, d in enumerate((2, 1, 3)):
            for h in range(2):
                put(self.sent.at[m, h], self.halves[h], self.row0 + (self.me + d) % 4 * self.n, self.n)
            self.copy(m).start()

    def last(self):
        for m in range(3):
            self.copy(m).wait()
        for h in range(2):
            add(self.halves[h], self.row0 + self.me * self.n, self.n, *[self.got.at[m, h] for m in range(3)])


class DirectGather:
    def __init__(self, remote, base, both, row0, n, me, ring):
        self.__dict__.update(locals())

    def copy(self, m):
        ref = self.both.at[:, pl.ds(aligned(self.row0 + self.me * self.n), self.n), :]
        return self.remote(self.base + m, ref, ref, self.ring[(2, 1, 3)[m]])

    def first(self):
        for m in range(3):
            self.copy(m).start()

    def last(self):
        for m in range(3):
            self.copy(m).wait()


def unit_scratch(kind, w):
    h, q = w // 2, w // 4
    if kind == 0:
        got = dict(first=(6, 64, h), second=(6, 16, h), y=(2, 16, h))
        own = dict(part=((2, 256, h), F32), pre=((2, 256, h), BF16))
    elif kind == 1:
        got = dict(first=(3, 2, 16, q), second=(6, 64, q))
        own = dict(part=((2, 256, q), F32), pre=((2, 2, 256, q), BF16), rows=((h, 128), BF16))
    else:
        got = dict(first=(6, 64, q), second=(6, 16, q))
        own = dict(part=((2, 256, q), F32), pre=((2, 256, h), BF16), rows=((h, 128), BF16))
    for name, shape in got.items():
        own["sent_" + name] = (shape, BF16)
        own["got_" + name] = (shape, BF16)
    own["send_sem"] = own["recv_sem"] = ((26,), None)
    return own


def kernel(qi_ref, qo_ref, a_hbm, g_hbm, x_hbm, o_hbm, out_ref, *scratch):
    (qs, qx, fac, inp, side, fin, rfin, fac_sem, inp_sem, q_send, q_recv, fin_send, fin_recv) = scratch[:13]
    rest = list(scratch[13:])
    bufs = [{name: rest.pop(0) for name in unit_scratch(kind, w)} for _, kind, _, w in UNITS]

    lay, tok = lax.axis_index("layer"), lax.axis_index("tok")
    core = lay % 2
    y = tok // 16
    step_p, step_s = 1 + 3 * core, 4 - 3 * core
    p, s = (tok // step_p) % 4, (tok // step_s) % 4

    def at(p_, s_, y_):
        return (lay, y_ * 16 + p_ * step_p + s_ * step_s)

    ring_p = [None] + [at((p + d) % 4, s, y) for d in (1, 2, 3)]
    ring_s = [None] + [at(p, (s + d) % 4, y) for d in (1, 2, 3)]
    across = at(p, s, 1 - y)
    peers = [((lay + d) % 4, tok) for d in (1, 2, 3)]

    def fac_copy(k):
        return pltpu.make_async_copy((a_hbm, g_hbm)[k % 2].at[k // 2], fac.at[k], fac_sem.at[k])

    def inp_copy(k):
        return pltpu.make_async_copy((x_hbm, o_hbm)[k % 2].at[k // 2], inp.at[k % 2], inp_sem.at[k])

    barrier = pltpu.get_barrier_semaphore()
    everyone = [*ring_p[1:], *ring_s[1:], across, *peers]
    for who in everyone:
        pl.semaphore_signal(barrier, inc=1, device_id=who, device_id_type=MESH)
    for k in range(SLABS):
        fac_copy(k).start()
    for k in range(2):
        inp_copy(k).start()
    for k in range(SLABS):
        qs[k] = (qi_ref, qo_ref)[k % 2][k // 2] * jnp.asarray(SCALE, BF16)

    log = []
    loaded, asked, arrived = set(), set(), set()

    def load(k):
        if k not in loaded:
            loaded.add(k)
            fac_copy(k).wait()

    def q_copy(k):
        return Remote(log, (q_send, q_recv), k, qs.at[k], qx.at[k], across)

    def dot(a, b):
        return lax.dot_general(a, b, NT, preferred_element_type=F32)

    waiting, scored = [], []

    def finish(u):
        waiting.append(u)
        for v in sorted(waiting):
            k = UNITS[v][0]
            if all(w in scored for w, unit in enumerate(UNITS) if unit[0] < k // 2 * 2):
                waiting.remove(v)
                take(v, k)

    def take(u, k):
        _, kind, col, w = UNITS[u]
        acc, data, pre = side.at[k % 2], inp.at[k % 2], bufs[u]["pre"]
        fresh = not any(UNITS[v][0] == k for v in scored)
        if fresh:
            inp_copy(k).wait()
        if kind == 1:
            pieces = [(pre[h // 2, h % 2], col + h * (w // 4), w // 4) for h in range(4)]
        else:
            pieces = [(pre[h], col + h * (w // 2), w // 2) for h in range(2)]
        for block, c, width in pieces:
            v = dot(data[:, pl.ds(c, width)], block)
            acc[...] = v if fresh else acc[...] + v
            fresh = False
        scored.append(u)
        if all(v in scored for v, unit in enumerate(UNITS) if unit[0] == k) and k + 2 < SLABS:
            inp_copy(k + 2).start()
        if all(v in scored for v, unit in enumerate(UNITS) if unit[0] // 2 == k // 2):
            layer_sum(k // 2)

    def layer_sum(layer):
        pick = jnp.where(
            lax.broadcasted_iota(jnp.int32, (32, 256), 1) // 8
            == lax.broadcasted_iota(jnp.int32, (32, 256), 0),
            1.0, 0.0,
        ).astype(BF16)
        for t in range(0, side.shape[1], 128):
            prod = side[0, pl.ds(t, 128), :] * side[1, pl.ds(t, 128), :]
            total = None
            for _ in range(3):
                top = prod.astype(BF16)
                prod = prod - top.astype(F32)
                part = dot(pick, top)
                total = part if total is None else total + part
            fin[:, pl.ds(t, 128)] = total if layer == 0 else fin[:, pl.ds(t, 128)] + total

    def exchange(u):
        k, _, col, w = UNITS[u]
        h = w // 2
        src = (a_hbm, g_hbm)[k % 2].at[k // 2, pl.ds(aligned(col + (1 - y) * h), h), :]
        return Remote(log, (bufs[u]["send_sem"], bufs[u]["recv_sem"]), 12, src, bufs[u]["rows"], across)

    def send_rows(u):
        k = UNITS[u][0]
        if k not in asked:
            asked.add(k)
            q_copy(k).start()
        exchange(u).start()

    def sum_rows(u):
        k, _, col, w = UNITS[u]
        load(k)
        if k not in arrived:
            arrived.add(k)
            q_copy(k).wait()
        exchange(u).wait()
        q, b = w // 4, bufs[u]
        for h in range(2):
            own = fac[k, pl.ds(aligned(col + y * (w // 2) + h * q), q), :]
            b["part"][h] = dot(qs[k], own) + dot(qx[k], b["rows"][pl.ds(h * q, q), :])

    def steps_of(u):
        k, kind, col, w = UNITS[u]
        b = bufs[u]
        part, pre, h, q = b["part"], b["pre"], w // 2, w // 4

        def remote(n, src, dst, who):
            return Remote(log, (b["send_sem"], b["recv_sem"]), n, src, dst, who)

        halves = [part.at[i] for i in range(2)]
        coded = lambda name: (b["sent_" + name], b["got_" + name])
        if kind == 0:
            one = Scatter(remote, 0, halves, *coded("first"), 0, 64, p, ring_p)
            two = Scatter(remote, 6, halves, *coded("second"), 64 * p, 16, s, ring_s)
            back_two = Gather(remote, 14, [pre.at[i] for i in range(2)], 64 * p, 16, s, ring_s)
            back_one = Gather(remote, 20, [pre.at[i] for i in range(2)], 0, 64, p, ring_p)
            row = 64 * p + 16 * s
            swap = remote(12, b["sent_y"], b["got_y"], across)

            def begin():
                load(k)
                for i in range(2):
                    part[i] = dot(qs[k], fac[k, pl.ds(col + i * h, h), :])
                one.first()

            def third():
                two.last()
                for i in range(2):
                    put(b["sent_y"].at[i], halves[i], row, 16)
                swap.start()

            def fourth():
                swap.wait()
                rows = pl.ds(aligned(row), 16)
                for i in range(2):
                    pre[i, rows, :] = ((part[i, rows, :] + decode(b["got_y"][i])) * (1.0 / SCALE)).astype(BF16)
                back_two.first()

            return [
                [begin], [one.second], [one.last, two.first], [two.second], [third], [fourth],
                [back_two.second], [back_two.last, back_one.first], [back_one.second],
                [back_one.last, lambda: finish(u)],
            ]
        if kind == 1:
            one = Scatter(remote, 0, halves, *coded("second"), 0, 64, s, ring_s)
            two = Direct(remote, 6, halves, *coded("first"), 64 * s, 16, p, ring_p)
            back_two = DirectGather(remote, 9, pre.at[y], 64 * s, 16, p, ring_p)
            back_one = Gather(remote, 20, [pre.at[y, i] for i in range(2)], 0, 64, s, ring_s)
            row = 64 * s + 16 * p
            swap = remote(13, pre.at[y], pre.at[y], across)

            def store():
                rows = pl.ds(aligned(row), 16)
                for i in range(2):
                    pre[y, i, rows, :] = (part[i, rows, :] * (1.0 / SCALE)).astype(BF16)

            return [
                [lambda: send_rows(u)], [lambda: sum_rows(u), one.first], [one.second],
                [one.last, two.first], [two.last, store, back_two.first], [back_two.last, back_one.first],
                [back_one.second], [back_one.last, swap.start], [swap.wait, lambda: finish(u)],
            ]
        one = Scatter(remote, 0, halves, *coded("first"), 0, 64, p, ring_p)
        two = Scatter(remote, 6, halves, *coded("second"), 64 * p, 16, s, ring_s)
        back_two = Gather(remote, 14, [pre.at[i] for i in range(2)], 64 * p, 16, s, ring_s)
        back_one = Gather(remote, 20, [pre.at[i] for i in range(2)], 0, 64, p, ring_p)
        rows = pl.ds(aligned(64 * p + 16 * s), 16)
        swap = remote(13, pre.at[y, rows, :], pre.at[y, rows, :], across)

        def store():
            for i in range(2):
                pre[y, rows, pl.ds(i * q, q)] = (part[i, rows, :] * (1.0 / SCALE)).astype(BF16)

        return [
            [lambda: send_rows(u)], [lambda: sum_rows(u), one.first], [one.second], [one.last, two.first],
            [two.second], [two.last, store, swap.start], [swap.wait, back_two.first], [back_two.second],
            [back_two.last, back_one.first], [back_one.second], [back_one.last, lambda: finish(u)],
        ]

    steps = [steps_of(u) for u in range(len(UNITS))]
    pl.semaphore_wait(barrier, len(everyone))
    for u in ORDER:
        for act in steps[u].pop(0):
            act()

    def fin_copy(d):
        who = (lay + d) % 4
        src = fin.at[pl.ds(pl.multiple_of(8 * who, 8), 8), :]
        return Remote(log, (fin_send, fin_recv), d - 1, src, rfin.at[d - 1], (who, tok))

    for d in (2, 3, 1):
        fin_copy(d).start()
    for c in log:
        c.wait_send()
    total = fin[pl.ds(pl.multiple_of(8 * lay, 8), 8), :]
    for d in (1, 2, 3):
        fin_copy(d).wait()
        total = total + rfin[d - 1]
    out_ref[...] = total


def local(inputs, out_grads, a_inverse, g_inverse, query_in, query_out):
    layers, tokens, width = inputs.shape
    depth = a_inverse.shape[2]
    rows = query_in.shape[1] * query_in.shape[2]
    dma = pltpu.SemaphoreType.DMA
    vmem = pltpu.VMEM
    scratch = [
        vmem((SLABS, rows, depth), BF16), vmem((SLABS, rows, depth), BF16),
        vmem((SLABS, width, depth), BF16), vmem((2, tokens, width), BF16),
        vmem((2, tokens, rows), F32), vmem((32, tokens), F32), vmem((3, 8, tokens), F32),
        dma((SLABS,)), dma((SLABS,)), dma((SLABS,)), dma((SLABS,)), dma((3,)), dma((3,)),
    ]
    for _, kind, _, w in UNITS:
        for shape, dtype in unit_scratch(kind, w).values():
            scratch.append(dma(shape) if dtype is None else vmem(shape, dtype))
    hbm = pl.BlockSpec(memory_space=pl.ANY)
    near = pl.BlockSpec(memory_space=pltpu.VMEM)
    scores = pl.pallas_call(
        kernel,
        out_shape=jax.ShapeDtypeStruct((8, tokens), F32),
        in_specs=[near, near, hbm, hbm, hbm, hbm],
        out_specs=near,
        scratch_shapes=scratch,
        compiler_params=pltpu.CompilerParams(
            collective_id=1, has_side_effects=True, vmem_limit_bytes=60 * 2**20
        ),
        cost_estimate=pl.CostEstimate(flops=6 * 10**9, bytes_accessed=26 * 10**6, transcendentals=0),
        name="influence",
    )(
        query_in.reshape(layers, rows, depth), query_out.reshape(layers, rows, depth),
        a_inverse, g_inverse, inputs, out_grads,
    )
    return scores.T


def solution(mesh):
    in_specs = (
        P("layer", "tok", None),
        P("layer", "tok", None),
        P("layer", None, "tok"),
        P("layer", None, "tok"),
        P("layer", None, None, "tok"),
        P("layer", None, None, "tok"),
    )
    return jax.shard_map(
        local, mesh=mesh, in_specs=in_specs, out_specs=P("tok", "layer"), check_vma=False
    )
```

time: 480 us -> 106 us (0.22)
  blocking collectives: 371 us -> 0 us
  Pallas kernels: 0 us -> 104 us
  waiting for transfers between devices: 39.9 us -> 0 us
  local copies, waits for them, and re-layouts: 29.4 us -> 1.34 us
  between operations: 14.3 us -> 0.01 us
  matrix products: 13.9 us -> 0 us
  other arithmetic: 12 us -> 0 us
    psum x1 -> x0, blocking collectives: 371 us -> none  [local(): lax.psum(jnp.concatenate([side_in.reshape(queries, half), side_out.reshap...]
    pallas_call x0 -> x1, Pallas kernels: none -> 104 us  [local(): pl.pallas_call(kernel, out_shape=jax.ShapeDtypeStruct((8, tokens), F32),...]
    unnamed x2 -> x0, waiting for transfers between devices: 39.9 us -> none
    unnamed x34 -> x1, local copies, waits for them, and re-layouts: 23.5 us -> 1.34 us
    dot_general x8 -> x0, matrix products: 13.9 us -> none  [the longest x4 6.21 us: precondition(): jnp.einsum('qrj,ij->qri', factors, inverse, preferred_element_type=jnp.fl...]
    concatenate x1 -> x0, other arithmetic: 9.44 us -> none  [local(): jnp.concatenate([side_in.reshape(queries, half), side_out.reshape(queries...]
  transfers between devices with their start and end apart: 1 -> 0, of which waited for: 1 -> 0; matrix products, arithmetic and copies ran while one was open for 0% -> 0% of each run, Pallas kernels for 0% -> 0%
where the time goes in v2:
time: 106 us; the launch traced here: 105 us
  Pallas kernels  104 us (98%)
  local copies, waits for them, and re-layouts  1.34 us (1%)
    pallas_call x1, Pallas kernels, local(): pl.pallas_call(kernel, out_shape=jax.ShapeDtypeStruct((8, tokens), F32),...  104 us

profile of v2, /device:TPU:1, one launch (start us, length us, event | category | flops | bytes accessed | tf_op | source)
XLA Modules:
  0.0 105.5 jit_solution(13136760808866716691)
XLA Ops:
  0.0 104.1 %influence.1 = f32[8,640]{1,0:T(8,128)} custom-call(bf16[2,256,128]{2,1,0:T(8,128)(2,1)} %bitcast.3, bf16[2,256,128]{2,1,0:T(8,128)(2,1)} %bitcast.4, bf16[2,4096,128]{2,1,0:T(8,128)(2,1)} %a_hbm.1, bf16[2,4096,128]{2,1,0:T(8,128)(2,1)} %g_hbm.1, bf16[2,640,4096]{2,1,0:T(8,128)(2,1)} %x_hbm.1, bf16[2,640,4096]{2,1,0:T(8,128)(2,1)} %o_hbm.1), custom_call_target="tpu_custom_call" | custom-call | flops 6000000000 | bytes 26000000 | tf_op jit(solution)/shard_map/influence/pallas_call | solution.py:443
  104.1 1.3 %copy.8 = f32[640,8]{0,1:T(8,128)} copy(f32[640,8]{0,1:T(8,128)} %bitcast.5) | data formatting | bytes 40960

commit v3 on v2

--- a/solution.py
+++ b/solution.py
@@ -13,24 +13,23 @@
 WEST, EAST = 3, 1
 
 UNITS = (
-    (0, 0, 0, 3072),
-    (0, 1, 3072, 1024),
-    (1, 0, 0, 2048),
-    (1, 1, 2048, 1024),
-    (1, 2, 3072, 1024),
-    (2, 0, 0, 2048),
-    (2, 1, 2048, 1024),
-    (2, 2, 3072, 1024),
-    (3, 0, 0, 2048),
-    (3, 1, 2048, 1024),
-    (3, 2, 3072, 1024),
+    (0, 0, 0, 2048, 0),
+    (0, 1, 2048, 1024, 0),
+    (0, 1, 3072, 1024, 0),
+    (1, 0, 0, 3072, 0),
+    (1, 1, 3072, 1024, 0),
+    (2, 0, 0, 512, 0),
+    (2, 2, 512, 2048, 0),
+    (2, 1, 2560, 1536, 0),
+    (3, 0, 0, 3072, 0),
+    (3, 1, 3072, 1024, 0),
 )
 
 ORDER = (
-    0, 1, 2, 3, 4, 5, 6, 7, 8, 9, 10, 0, 1, 2, 1, 3, 5, 1, 4, 3, 8, 6, 3, 0, 2, 5, 6, 1, 4, 7,
-    0, 2, 8, 9, 5, 3, 1, 4, 6, 7, 0, 2, 8, 10, 9, 3, 5, 1, 6, 7, 4, 8, 10, 0, 9, 3, 2, 1, 7, 4,
-    5, 6, 10, 0, 8, 3, 9, 2, 7, 5, 6, 10, 0, 8, 2, 9, 5, 1, 4, 6, 10, 8, 9, 4, 0, 3, 7, 9, 4, 2,
-    7, 5, 6, 10, 7, 8, 10, 9, 0, 4, 10, 2, 5, 7, 8, 4, 10, 7, 10,
+    1, 0, 3, 4, 0, 6, 1, 7, 2, 8, 1, 9, 4, 0, 1, 4, 3, 8, 6, 0, 5, 0, 4, 3, 1, 7, 6, 8, 5, 3,
+    2, 4, 7, 1, 8, 6, 9, 5, 3, 0, 2, 1, 7, 8, 6, 4, 9, 5, 0, 3, 2, 1, 7, 4, 6, 8, 9, 3, 5, 0,
+    7, 9, 4, 2, 8, 3, 7, 6, 1, 2, 8, 7, 9, 0, 5, 2, 6, 9, 2, 5, 9, 6, 3, 0, 5, 4, 8, 2, 7, 6,
+    3, 5, 8, 9, 6, 5,
 )
 
 
@@ -149,6 +148,8 @@
 
 
 class Direct:
+    second = None
+
     def __init__(self, remote, base, halves, sent, got, row0, n, me, ring):
         self.__dict__.update(locals())
 
@@ -169,6 +170,8 @@
 
 
 class DirectGather:
+    second = None
+
     def __init__(self, remote, base, both, row0, n, me, ring):
         self.__dict__.update(locals())
 
@@ -185,16 +188,16 @@
             self.copy(m).wait()
 
 
-def unit_scratch(kind, w):
+def unit_scratch(kind, w, straight):
     h, q = w // 2, w // 4
     if kind == 0:
-        got = dict(first=(6, 64, h), second=(6, 16, h), y=(2, 16, h))
+        got = dict(first=(6, 64, h), second=(3, 2, 16, h) if straight & 2 else (6, 16, h), y=(2, 16, h))
         own = dict(part=((2, 256, h), F32), pre=((2, 256, h), BF16))
     elif kind == 1:
         got = dict(first=(3, 2, 16, q), second=(6, 64, q))
         own = dict(part=((2, 256, q), F32), pre=((2, 2, 256, q), BF16), rows=((h, 128), BF16))
     else:
-        got = dict(first=(6, 64, q), second=(6, 16, q))
+        got = dict(first=(6, 64, q), second=(3, 2, 16, q) if straight & 2 else (6, 16, q))
         own = dict(part=((2, 256, q), F32), pre=((2, 256, h), BF16), rows=((h, 128), BF16))
     for name, shape in got.items():
         own["sent_" + name] = (shape, BF16)
@@ -206,7 +209,7 @@
 def kernel(qi_ref, qo_ref, a_hbm, g_hbm, x_hbm, o_hbm, out_ref, *scratch):
     (qs, qx, fac, inp, side, fin, rfin, fac_sem, inp_sem, q_send, q_recv, fin_send, fin_recv) = scratch[:13]
     rest = list(scratch[13:])
-    bufs = [{name: rest.pop(0) for name in unit_scratch(kind, w)} for _, kind, _, w in UNITS]
+    bufs = [{name: rest.pop(0) for name in unit_scratch(kind, w, straight)} for _, kind, _, w, straight in UNITS]
 
     lay, tok = lax.axis_index("layer"), lax.axis_index("tok")
     core = lay % 2
@@ -264,7 +267,7 @@
                 take(v, k)
 
     def take(u, k):
-        _, kind, col, w = UNITS[u]
+        _, kind, col, w, _ = UNITS[u]
         acc, data, pre = side.at[k % 2], inp.at[k % 2], bufs[u]["pre"]
         fresh = not any(UNITS[v][0] == k for v in scored)
         if fresh:
@@ -300,7 +303,7 @@
             fin[:, pl.ds(t, 128)] = total if layer == 0 else fin[:, pl.ds(t, 128)] + total
 
     def exchange(u):
-        k, _, col, w = UNITS[u]
+        k, _, col, w, _ = UNITS[u]
         h = w // 2
         src = (a_hbm, g_hbm)[k % 2].at[k // 2, pl.ds(aligned(col + (1 - y) * h), h), :]
         return Remote(log, (bufs[u]["send_sem"], bufs[u]["recv_sem"]), 12, src, bufs[u]["rows"], across)
@@ -313,7 +316,7 @@
         exchange(u).start()
 
     def sum_rows(u):
-        k, _, col, w = UNITS[u]
+        k, _, col, w, _ = UNITS[u]
         load(k)
         if k not in arrived:
             arrived.add(k)
@@ -325,7 +328,7 @@
             b["part"][h] = dot(qs[k], own) + dot(qx[k], b["rows"][pl.ds(h * q, q), :])
 
     def steps_of(u):
-        k, kind, col, w = UNITS[u]
+        k, kind, col, w, straight = UNITS[u]
         b = bufs[u]
         part, pre, h, q = b["part"], b["pre"], w // 2, w // 4
 
@@ -333,12 +336,17 @@
             return Remote(log, (b["send_sem"], b["recv_sem"]), n, src, dst, who)
 
         halves = [part.at[i] for i in range(2)]
+        def gather(direct, base, both, row0, n, me, ring):
+            if direct:
+                return DirectGather(remote, base, both, row0, n, me, ring)
+            return Gather(remote, base, [both.at[i] for i in range(2)], row0, n, me, ring)
+
         coded = lambda name: (b["sent_" + name], b["got_" + name])
         if kind == 0:
             one = Scatter(remote, 0, halves, *coded("first"), 0, 64, p, ring_p)
-            two = Scatter(remote, 6, halves, *coded("second"), 64 * p, 16, s, ring_s)
-            back_two = Gather(remote, 14, [pre.at[i] for i in range(2)], 64 * p, 16, s, ring_s)
-            back_one = Gather(remote, 20, [pre.at[i] for i in range(2)], 0, 64, p, ring_p)
+            two = (Direct if straight & 2 else Scatter)(remote, 6, halves, *coded("second"), 64 * p, 16, s, ring_s)
+            back_two = gather(straight & 2, 14, pre, 64 * p, 16, s, ring_s)
+            back_one = gather(straight & 1, 20, pre, 0, 64, p, ring_p)
             row = 64 * p + 16 * s
             swap = remote(12, b["sent_y"], b["got_y"], across)
 
@@ -370,7 +378,7 @@
             one = Scatter(remote, 0, halves, *coded("second"), 0, 64, s, ring_s)
             two = Direct(remote, 6, halves, *coded("first"), 64 * s, 16, p, ring_p)
             back_two = DirectGather(remote, 9, pre.at[y], 64 * s, 16, p, ring_p)
-            back_one = Gather(remote, 20, [pre.at[y, i] for i in range(2)], 0, 64, s, ring_s)
+            back_one = gather(straight & 1, 20, pre.at[y], 0, 64, s, ring_s)
             row = 64 * s + 16 * p
             swap = remote(13, pre.at[y], pre.at[y], across)
 
@@ -385,9 +393,9 @@
                 [back_one.second], [back_one.last, swap.start], [swap.wait, lambda: finish(u)],
             ]
         one = Scatter(remote, 0, halves, *coded("first"), 0, 64, p, ring_p)
-        two = Scatter(remote, 6, halves, *coded("second"), 64 * p, 16, s, ring_s)
-        back_two = Gather(remote, 14, [pre.at[i] for i in range(2)], 64 * p, 16, s, ring_s)
-        back_one = Gather(remote, 20, [pre.at[i] for i in range(2)], 0, 64, p, ring_p)
+        two = (Direct if straight & 2 else Scatter)(remote, 6, halves, *coded("second"), 64 * p, 16, s, ring_s)
+        back_two = gather(straight & 2, 14, pre, 64 * p, 16, s, ring_s)
+        back_one = gather(straight & 1, 20, pre, 0, 64, p, ring_p)
         rows = pl.ds(aligned(64 * p + 16 * s), 16)
         swap = remote(13, pre.at[y, rows, :], pre.at[y, rows, :], across)
 
@@ -401,7 +409,7 @@
             [back_two.last, back_one.first], [back_one.second], [back_one.last, lambda: finish(u)],
         ]
 
-    steps = [steps_of(u) for u in range(len(UNITS))]
+    steps = [[acts for acts in steps_of(u) if acts != [None]] for u in range(len(UNITS))]
     pl.semaphore_wait(barrier, len(everyone))
     for u in ORDER:
         for act in steps[u].pop(0):
@@ -435,8 +443,8 @@
         vmem((2, tokens, rows), F32), vmem((32, tokens), F32), vmem((3, 8, tokens), F32),
         dma((SLABS,)), dma((SLABS,)), dma((SLABS,)), dma((SLABS,)), dma((3,)), dma((3,)),
     ]
-    for _, kind, _, w in UNITS:
-        for shape, dtype in unit_scratch(kind, w).values():
+    for _, kind, _, w, straight in UNITS:
+        for shape, dtype in unit_scratch(kind, w, straight).values():
             scratch.append(dma(shape) if dtype is None else vmem(shape, dtype))
     hbm = pl.BlockSpec(memory_space=pl.ANY)
     near = pl.BlockSpec(memory_space=pltpu.VMEM)

time: 106 us -> 97.2 us (0.917)
  Pallas kernels: 104 us -> 95.7 us
    pallas_call x1, Pallas kernels: 104 us -> 95.7 us  [local(): pl.pallas_call(kernel, out_shape=jax.ShapeDtypeStruct((8, tokens), F32),...]
where the time goes in v3:
time: 97.2 us; the launch traced here: 97 us
  Pallas kernels  95.7 us (98%)
  local copies, waits for them, and re-layouts  1.34 us (1%)
    pallas_call x1, Pallas kernels, local(): pl.pallas_call(kernel, out_shape=jax.ShapeDtypeStruct((8, tokens), F32),...  95.7 us

profile of v3, /device:TPU:1, one launch (start us, length us, event | category | flops | bytes accessed | tf_op | source)
XLA Modules:
  0.0 97.0 jit_solution(17735178339252092789)
XLA Ops:
  0.0 95.7 %influence.1 = f32[8,640]{1,0:T(8,128)} custom-call(bf16[2,256,128]{2,1,0:T(8,128)(2,1)} %bitcast.3, bf16[2,256,128]{2,1,0:T(8,128)(2,1)} %bitcast.4, bf16[2,4096,128]{2,1,0:T(8,128)(2,1)} %a_hbm.1, bf16[2,4096,128]{2,1,0:T(8,128)(2,1)} %g_hbm.1, bf16[2,640,4096]{2,1,0:T(8,128)(2,1)} %x_hbm.1, bf16[2,640,4096]{2,1,0:T(8,128)(2,1)} %o_hbm.1), custom_call_target="tpu_custom_call" | custom-call | flops 6000000000 | bytes 26000000 | tf_op jit(solution)/shard_map/influence/pallas_call | solution.py:451
  95.7 1.3 %copy.8 = f32[640,8]{0,1:T(8,128)} copy(f32[640,8]{0,1:T(8,128)} %bitcast.5) | data formatting | bytes 40960

commit v4 on v3

--- a/solution.py
+++ b/solution.py
@@ -10,26 +10,25 @@
 SCALE = 2.0**29
 NT = (((1,), (1,)), ((), ()))
 SLABS = 4
+LATE = 10
 WEST, EAST = 3, 1
 
 UNITS = (
     (0, 0, 0, 2048, 0),
-    (0, 1, 2048, 1024, 0),
-    (0, 1, 3072, 1024, 0),
+    (0, 1, 2048, 2048, 0),
     (1, 0, 0, 3072, 0),
     (1, 1, 3072, 1024, 0),
     (2, 0, 0, 512, 0),
     (2, 2, 512, 2048, 0),
     (2, 1, 2560, 1536, 0),
     (3, 0, 0, 3072, 0),
-    (3, 1, 3072, 1024, 0),
+    (3, 1, 3072, 1024, 1),
 )
 
 ORDER = (
-    1, 0, 3, 4, 0, 6, 1, 7, 2, 8, 1, 9, 4, 0, 1, 4, 3, 8, 6, 0, 5, 0, 4, 3, 1, 7, 6, 8, 5, 3,
-    2, 4, 7, 1, 8, 6, 9, 5, 3, 0, 2, 1, 7, 8, 6, 4, 9, 5, 0, 3, 2, 1, 7, 4, 6, 8, 9, 3, 5, 0,
-    7, 9, 4, 2, 8, 3, 7, 6, 1, 2, 8, 7, 9, 0, 5, 2, 6, 9, 2, 5, 9, 6, 3, 0, 5, 4, 8, 2, 7, 6,
-    3, 5, 8, 9, 6, 5,
+    4, 0, 1, 3, 5, 2, 6, 7, 0, 1, 2, 4, 7, 3, 1, 3, 8, 0, 1, 5, 4, 2, 0, 3, 4, 7, 6, 1, 5, 2,
+    0, 7, 8, 3, 1, 6, 4, 5, 0, 2, 8, 7, 1, 3, 6, 5, 0, 2, 4, 1, 8, 3, 7, 5, 6, 2, 0, 4, 8, 3,
+    7, 6, 2, 0, 4, 7, 6, 8, 2, 1, 5, 6, 8, 5, 4, 5, 7, 3, 0, 2, 5, 4, 6, 7, 8, 5,
 )
 
 
@@ -237,8 +236,6 @@
         pl.semaphore_signal(barrier, inc=1, device_id=who, device_id_type=MESH)
     for k in range(SLABS):
         fac_copy(k).start()
-    for k in range(2):
-        inp_copy(k).start()
     for k in range(SLABS):
         qs[k] = (qi_ref, qo_ref)[k % 2][k // 2] * jnp.asarray(SCALE, BF16)
 
@@ -411,9 +408,11 @@
 
     steps = [[acts for acts in steps_of(u) if acts != [None]] for u in range(len(UNITS))]
     pl.semaphore_wait(barrier, len(everyone))
-    for u in ORDER:
+    for i, u in enumerate(ORDER):
         for act in steps[u].pop(0):
             act()
+        if i in (LATE, LATE + 4):
+            inp_copy((i - LATE) // 4).start()
 
     def fin_copy(d):
         who = (lay + d) % 4

time: 97.2 us -> 94.9 us (0.976)
  Pallas kernels: 95.7 us -> 93.4 us
    pallas_call x1, Pallas kernels: 95.7 us -> 93.4 us  [local(): pl.pallas_call(kernel, out_shape=jax.ShapeDtypeStruct((8, tokens), F32),...]
where the time goes in v4:
time: 94.9 us; the launch traced here: 94.7 us
  Pallas kernels  93.4 us (98%)
  local copies, waits for them, and re-layouts  1.34 us (1%)
    pallas_call x1, Pallas kernels, local(): pl.pallas_call(kernel, out_shape=jax.ShapeDtypeStruct((8, tokens), F32),...  93.4 us

profile of v4, /device:TPU:1, one launch (start us, length us, event | category | flops | bytes accessed | tf_op | source)
XLA Modules:
  0.0 94.7 jit_solution(2740759304533885457)
XLA Ops:
  0.0 93.4 %influence.1 = f32[8,640]{1,0:T(8,128)} custom-call(bf16[2,256,128]{2,1,0:T(8,128)(2,1)} %bitcast.3, bf16[2,256,128]{2,1,0:T(8,128)(2,1)} %bitcast.4, bf16[2,4096,128]{2,1,0:T(8,128)(2,1)} %a_hbm.1, bf16[2,4096,128]{2,1,0:T(8,128)(2,1)} %g_hbm.1, bf16[2,640,4096]{2,1,0:T(8,128)(2,1)} %x_hbm.1, bf16[2,640,4096]{2,1,0:T(8,128)(2,1)} %o_hbm.1), custom_call_target="tpu_custom_call" | custom-call | flops 6000000000 | bytes 26000000 | tf_op jit(solution)/shard_map/influence/pallas_call | solution.py:450
  93.4 1.3 %copy.8 = f32[640,8]{0,1:T(8,128)} copy(f32[640,8]{0,1:T(8,128)} %bitcast.5) | data formatting | bytes 40960

commit v5 on v4

--- a/solution.py
+++ b/solution.py
@@ -230,15 +230,16 @@
     def inp_copy(k):
         return pltpu.make_async_copy((x_hbm, o_hbm)[k % 2].at[k // 2], inp.at[k % 2], inp_sem.at[k])
 
+    fac_copy(0).start()
     barrier = pltpu.get_barrier_semaphore()
     everyone = [*ring_p[1:], *ring_s[1:], across, *peers]
     for who in everyone:
         pl.semaphore_signal(barrier, inc=1, device_id=who, device_id_type=MESH)
     for k in range(SLABS):
+        qs[k] = (qi_ref, qo_ref)[k % 2][k // 2] * jnp.asarray(SCALE, BF16)
+
+    for k in range(1, SLABS):
         fac_copy(k).start()
-    for k in range(SLABS):
-        qs[k] = (qi_ref, qo_ref)[k % 2][k // 2] * jnp.asarray(SCALE, BF16)
-
     log = []
     loaded, asked, arrived = set(), set(), set()
 

time: 94.9 us -> 94.9 us (level)
  no operation moved by 1% of the time
where the time goes in v5:
time: 94.9 us; the launch traced here: 94.7 us
  Pallas kernels  93.4 us (98%)
  local copies, waits for them, and re-layouts  1.34 us (1%)
    pallas_call x1, Pallas kernels, local(): pl.pallas_call(kernel, out_shape=jax.ShapeDtypeStruct((8, tokens), F32),...  93.4 us

profile of v5, /device:TPU:1, one launch (start us, length us, event | category | flops | bytes accessed | tf_op | source)
XLA Modules:
  0.0 94.7 jit_solution(15960768061968469972)
XLA Ops:
  0.0 93.4 %influence.1 = f32[8,640]{1,0:T(8,128)} custom-call(bf16[2,256,128]{2,1,0:T(8,128)(2,1)} %bitcast.3, bf16[2,256,128]{2,1,0:T(8,128)(2,1)} %bitcast.4, bf16[2,4096,128]{2,1,0:T(8,128)(2,1)} %a_hbm.1, bf16[2,4096,128]{2,1,0:T(8,128)(2,1)} %g_hbm.1, bf16[2,640,4096]{2,1,0:T(8,128)(2,1)} %x_hbm.1, bf16[2,640,4096]{2,1,0:T(8,128)(2,1)} %o_hbm.1), custom_call_target="tpu_custom_call" | custom-call | flops 6000000000 | bytes 26000000 | tf_op jit(solution)/shard_map/influence/pallas_call | solution.py:451
  93.4 1.3 %copy.8 = f32[640,8]{0,1:T(8,128)} copy(f32[640,8]{0,1:T(8,128)} %bitcast.5) | data formatting | bytes 40960
